TPU v7x, 32 devices: a whole 2x2x4 slice. The times are simulated.
32 devices in a mesh: dp: 4 (over z), proto: 8 (over y, x, core).
Axes of the slice: x: 2, y: 2, z: 4, core: 2. Of those that a mesh axis runs over, the one named last changes fastest.
Arguments:
- embeddings: bfloat16 [8192, 2560], P('proto', 'dp'), may hold values from -26 to 26
- table: bfloat16 [32768, 2560], P('proto', 'dp'), may hold values from -5 to 5
- tile_lists: int32 [8, 8], replicated, may hold values from 0 to 255, as said below
- labels: int32 [8192], P('proto'), may hold values from 0 to 32767, as said below
Outputs:
- loss: float32 [], replicated
- grad_emb: bfloat16 [8192, 2560], P('proto', 'dp')
- grad_table: bfloat16 [32768, 2560], P('proto', 'dp')
Inputs may be any that keep to these rules, and one draw needn't show every extreme that they name: `tile_lists`: each block's 8 tile ids are distinct and fall on exactly 4 owners (owner = id // 32), each of those owners holding exactly 2 of them. `labels`: the tile of each row's label (label // 128) is in the list of the row's block.
All inputs are finite; a program needn't handle non-finite values.
Results may differ from a plain program's by a relative error of at most 0.0025.
The roundings to bfloat16 on the way count: a program that leaves them out, or rounds other values in their place, can miss the bound.
Values may be sent and summed in bfloat16 or wider, within the bound.
A program may use at most 128 MiB of HBM per device.

v0:
```python
import math
import jax
import jax.numpy as jnp
from jax import lax
from jax.sharding import PartitionSpec as P

D = 2560
TILE = 128
CAP = 2


def slot_plan(ids, tiles_here):
    owners = ids // tiles_here
    local = ids % tiles_here
    count = ids.shape[-1]
    before = jnp.arange(count)[:, None] > jnp.arange(count)[None, :]
    earlier = (owners[..., :, None] == owners[..., None, :]) & before
    rank = jnp.sum(earlier.astype(jnp.int32), axis=-1)
    return (owners, local, rank)


def softmax_terms(scores, ids, lab, list_len):
    hit = (ids[None, :] == (lab // TILE)[:, None]).astype(jnp.int32)
    column = (
        jnp.sum(hit * (jnp.arange(list_len, dtype=jnp.int32) * TILE)[None, :], axis=1) + lab % TILE
    )
    onehot = (jnp.arange(list_len * TILE, dtype=jnp.int32)[None, :] == column[:, None]).astype(
        jnp.float32
    )
    top = jnp.max(scores, axis=1, keepdims=True)
    expo = jnp.exp(scores - top)
    total = jnp.sum(expo, axis=1, keepdims=True)
    lse = top[:, 0] + jnp.log(total[:, 0])
    target = jnp.sum(scores * onehot, axis=1)
    dz_rows = (expo / total - onehot).astype(jnp.bfloat16)
    return (jnp.sum(lse - target), dz_rows)


def body(embeddings, table, tile_lists, labels):
    block_rows, width = embeddings.shape
    list_len = tile_lists.shape[1]
    tiles_here = table.shape[0] // TILE
    groups = lax.axis_size("proto")
    dp_count = lax.axis_size("dp")
    rows_dev = block_rows // dp_count
    total_rows = block_rows * groups
    me = lax.axis_index("proto")
    part = lax.axis_index("dp")
    inv_scale = 1.0 / math.sqrt(D)
    owners, local, rank = slot_plan(tile_lists, tiles_here)
    match = (owners == me)[:, :, None] & (
        rank[:, :, None] == jnp.arange(CAP, dtype=jnp.int32)[None, None, :]
    )
    select = jnp.sum(match.astype(jnp.int32) * local[:, :, None], axis=1)
    shaped_table = table.reshape(tiles_here, TILE, width)
    outgoing = jnp.take(shaped_table, select.reshape(-1), axis=0).reshape(groups, CAP, TILE, width)
    incoming = lax.all_to_all(outgoing, "proto", split_axis=0, concat_axis=0, tiled=True)
    my_ids = lax.dynamic_index_in_dim(tile_lists, me, 0, keepdims=False)
    my_owner = lax.dynamic_index_in_dim(owners, me, 0, keepdims=False)
    my_rank = lax.dynamic_index_in_dim(rank, me, 0, keepdims=False)
    flat_slot = my_owner * CAP + my_rank
    tiles = jnp.take(incoming.reshape(groups * CAP, TILE, width), flat_slot, axis=0).reshape(
        list_len * TILE, width
    )
    scores = (
        lax.psum_scatter(
            lax.dot_general(
                embeddings, tiles, (((1,), (1,)), ((), ())), preferred_element_type=jnp.float32
            ),
            "dp",
            scatter_dimension=0,
            tiled=True,
        )
        * inv_scale
    )
    my_labels = lax.dynamic_slice_in_dim(labels, part * rows_dev, rows_dev, 0)
    loss_part, dz_rows = softmax_terms(scores, my_ids, my_labels, list_len)
    dz_block = lax.all_gather(dz_rows, "dp", axis=0, tiled=True)
    loss = lax.psum(loss_part, ("dp", "proto")) / total_rows
    grad_emb = jnp.dot(dz_block, tiles, preferred_element_type=jnp.float32).astype(jnp.bfloat16)
    piece = lax.dot_general(
        dz_block, embeddings, (((0,), (0,)), ((), ())), preferred_element_type=jnp.float32
    ).astype(jnp.bfloat16)
    returning = (
        jnp.zeros((groups * CAP, TILE, width), jnp.bfloat16)
        .at[flat_slot]
        .set(piece.reshape(list_len, TILE, width))
    )
    returned = lax.all_to_all(
        returning.reshape(groups, CAP, TILE, width),
        "proto",
        split_axis=0,
        concat_axis=0,
        tiled=True,
    )
    accum = (
        jnp.zeros((tiles_here, TILE, width), jnp.float32)
        .at[select.reshape(-1)]
        .add(returned.reshape(groups * CAP, TILE, width))
    )
    grad_table = accum.reshape(tiles_here * TILE, width).astype(jnp.bfloat16)
    return (loss, grad_emb, grad_table)


def solution(mesh):
    placed = (P("proto", "dp"), P("proto", "dp"), P(), P("proto"))
    return jax.shard_map(
        body,
        mesh=mesh,
        in_specs=placed,
        out_specs=(P(), P("proto", "dp"), P("proto", "dp")),
        check_vma=False,
    )
```

profile of v0, /device:TPU:0, one launch (start us, length us, event | category | flops | bytes accessed | tf_op | source)
XLA Modules:
  0.0 308.0 jit_solution(9859530231807013274)
XLA Ops:
  7.2 0.8 add_select_fusion
  8.0 0.7 broadcast_compare_fusion
  8.7 0.3 convert_reduce_fusion
  9.0 0.2 select_reduce_fusion.2
  9.2 0.1 copy.7
  9.4 4.8 %gather_fusion = bf16[16,128,640]{2,1,0:T(8,128)(2,1)} fusion(bf16[32,128,640]{2,1,0:T(8,128)(2,1)} %bitcast.36, s32[1024]{0:T(1024)S(1)} %pad_clamp_fusion.1), kind=kCustom, calls=%fused_computation | custom fusion | bytes 5242944 | tf_op jit(solution)/shard_map/jit(_take)/gather | solution.py:56
  14.3 3.6 %broadcast_select_fusion = bf16[8,2,128,640]{3,2,1,0:T(8,128)(2,1)} fusion(bf16[8,2,128,640]{3,2,1,0:T(8,128)(2,1)} %bitcast.33, pred[8,2]{1,0:T(8,128)(4,1)S(1)} %copy.7), kind=kLoop, calls=%fused_computation.5 | loop fusion | flops 1310720 | bytes 5242896 | tf_op jit(solution)/shard_map/jit(_take)/select_n | solution.py:56
  17.8 5.2 %all-to-all-start = ((bf16[8,2,128,640]{3,2,1,0:T(8,128)(2,1)}), bf16[8,2,128,640]{3,2,1,0:T(8,128)(2,1)}, u32[]{:S(2)}, u32[]{:S(2)}) async-start(bf16[8,2,128,640]{3,2,1,0:T(8,128)(2,1)} %broadcast_select_fusion), calls=%async_computation | async-start | bytes 5242880 | tf_op jit(solution)/shard_map/all_to_all | solution.py:57
  23.2 32.2 %all-to-all-done = bf16[8,2,128,640]{3,2,1,0:T(8,128)(2,1)} async-done(((bf16[8,2,128,640]{3,2,1,0:T(8,128)(2,1)}), bf16[8,2,128,640]{3,2,1,0:T(8,128)(2,1)}, u32[]{:S(2)}, u32[]{:S(2)}) %all-to-all-start) | async-done | bytes 2621472 | tf_op jit(solution)/shard_map/all_to_all | solution.py:57
  55.4 2.5 gather_fusion.1
  57.9 0.3 bitcast_select_fusion
  58.2 1.0 copy-done.2
  59.3 3.8 %convolution_bitcast_fusion = f32[1024,1024]{0,1:T(8,128)} fusion(bf16[1024,640]{1,0:T(8,128)(2,1)S(1)} %bitcast_select_fusion, bf16[1024,640]{1,0:T(8,128)(2,1)S(1)} %copy-done), kind=kOutput, calls=%fused_computation.6 | convolution fusion | flops 1342177280 | bytes 6815744 | tf_op jit(solution)/shard_map/dot_general | solution.py:67
  63.2 0.7 fusion.7
  64.0 0.1 select_reduce_fusion.1
  64.1 0.1 fusion.4
  64.2 75.9 %reduce-scatter.2.cloned.1.call-done = f32[256,1024]{0,1:T(8,128)} async-done(((f32[1024,1024]{0,1:T(8,128)}), f32[256,1024]{0,1:T(8,128)}) %reduce-scatter.2.cloned.1.call-update) | async-done | bytes 1048592 | tf_op jit(solution)/shard_map/reduce_scatter | solution.py:66
  140.1 1.5 multiply_reduce_fusion
  141.6 1.5 fusion
  143.1 1.1 subtract_convert_fusion
  144.3 46.9 %all-gather.2.cloned.1.call-done = bf16[1024,1024]{0,1:T(8,128)(2,1)} async-done(((bf16[256,1024]{0,1:T(8,128)(2,1)}), bf16[1024,1024]{0,1:T(8,128)(2,1)}) %all-gather.2.cloned.1.call-update) | async-done | bytes 2097168 | tf_op jit(solution)/shard_map/all_gather | solution.py:78
  191.2 3.4 %convolution_convert_fusion = bf16[1024,640]{1,0:T(8,128)(2,1)S(1)} fusion(bf16[1024,1024]{0,1:T(8,128)(2,1)} %all-gather.2.cloned.1.call-done, bf16[1024,640]{1,0:T(8,128)(2,1)S(1)} %copy-done), kind=kOutput, calls=%fused_computation.7 | convolution fusion | flops 1342832640 | bytes 4718592 | tf_op jit(solution)/shard_map/dot_general | solution.py:81
  194.6 1.8 broadcast_in_dim.55
  196.4 3.1 scatter_fusion
  199.4 4.5 %all-to-all-start.1 = ((bf16[8,2,128,640]{3,2,1,0:T(8,128)(2,1)}), bf16[8,2,128,640]{3,2,1,0:T(8,128)(2,1)}, u32[]{:S(2)}, u32[]{:S(2)}) async-start(bf16[8,2,128,640]{3,2,1,0:T(8,128)(2,1)} %bitcast.32), calls=%async_computation.2 | async-start | bytes 5242880 | tf_op jit(solution)/shard_map/all_to_all | solution.py:89
  203.9 0.6 subtract_reduce_fusion
  204.5 62.9 %psum.7 = f32[]{:T(128)} all-reduce(f32[]{:T(128)} %subtract_reduce_fusion), channel_id=1, replica_groups=mesh['dp'=4,'proto'=8] {'dp','proto'}, use_global_device_ids=true, to_apply=%region_8.9 | all-reduce | flops 1 | bytes 8 | tf_op jit(solution)/shard_map/psum | solution.py:79
  268.1 4.5 %convolution_convert_fusion.1 = bf16[1024,640]{1,0:T(8,128)(2,1)} fusion(bf16[1024,1024]{0,1:T(8,128)(2,1)} %all-gather.2.cloned.1.call-done, bf16[1024,640]{1,0:T(8,128)(2,1)S(1)} %copy-done.3), kind=kOutput, calls=%fused_computation.8 | convolution fusion | flops 1342832640 | bytes 4718592 | tf_op jit(solution)/shard_map/dot_general | solution.py:80
  272.6 4.6 %bitcast_convert_fusion = f32[16,128,640]{2,1,0:T(8,128)} fusion(bf16[8,2,128,640]{3,2,1,0:T(8,128)(2,1)} %all-to-all-done.1), kind=kLoop, calls=%fused_computation.4 | loop fusion | flops 1310720 | bytes 7864320 | tf_op jit(solution)/shard_map/convert_element_type | solution.py:99
  277.3 5.2 %broadcast_in_dim.54 = f32[32,128,640]{2,1,0:T(8,128)} broadcast(f32[]{:T(128)} %constant.115.clone.1), dimensions={} | broadcast | bytes 10485764 | tf_op jit(solution)/shard_map/broadcast_in_dim | solution.py:97
  282.5 10.5 %scatter_fusion.1 = f32[32,128,640]{2,1,0:T(8,128)} fusion(f32[32,128,640]{2,1,0:T(8,128)} %broadcast_in_dim.54, s32[16]{0:T(128)S(1)} %fusion.8, f32[16,128,640]{2,1,0:T(8,128)} %bitcast_convert_fusion), kind=kCustom, calls=%fused_computation.3 | custom fusion | flops 1310720 | bytes 15728704 | tf_op jit(solution)/shard_map/scatter-add | solution.py:99
  292.9 7.1 %convert_element_type.36 = bf16[32,128,640]{2,1,0:T(8,128)(2,1)} convert(f32[32,128,640]{2,1,0:T(8,128)} %scatter_fusion.1) | non-fusion elementwise | flops 2621440 | bytes 15728640 | tf_op jit(solution)/shard_map/convert_element_type | solution.py:101
  (25 shorter events, 0.5 us)
Async XLA Ops:
  7.2 52.1 %copy-start = (bf16[1024,640]{1,0:T(8,128)(2,1)S(1)}, bf16[1024,640]{1,0:T(8,128)(2,1)}, u32[]{:S(2)}) copy-start(bf16[1024,640]{1,0:T(8,128)(2,1)} %param.4) | copy-start | bytes 3932164
  17.8 37.5 %all-to-all-start = ((bf16[8,2,128,640]{3,2,1,0:T(8,128)(2,1)}), bf16[8,2,128,640]{3,2,1,0:T(8,128)(2,1)}, u32[]{:S(2)}, u32[]{:S(2)}) async-start(bf16[8,2,128,640]{3,2,1,0:T(8,128)(2,1)} %broadcast_select_fusion), calls=%async_computation | async-start | bytes 5242880 | tf_op jit(solution)/shard_map/all_to_all | solution.py:57
  23.0 117.1 %reduce-scatter.2.cloned.1.call-start = ((), (), s32[]{:S(2)}) async-start(), calls=%async_computation.3 | async-start | bytes 5242880 | tf_op jit(solution)/shard_map/reduce_scatter | solution.py:66
  58.2 1.1 copy-start.2
  63.1 0.8 copy-start.4
  63.2 128.0 %all-gather.2.cloned.1.call-start = ((), (), s32[]{:S(2)}) async-start(), calls=%async_computation.4 | async-start | bytes 2621440 | tf_op jit(solution)/shard_map/all_gather | solution.py:78
  140.1 3.0 copy-start.1
  199.4 68.7 %copy-start.3 = (bf16[1024,640]{1,0:T(8,128)(2,1)S(1)}, bf16[1024,640]{1,0:T(8,128)(2,1)}, u32[]{:S(2)}) copy-start(bf16[1024,640]{1,0:T(8,128)(2,1)} %copy-done.2) | copy-start | bytes 3932164
  199.4 73.2 %all-to-all-start.1 = ((bf16[8,2,128,640]{3,2,1,0:T(8,128)(2,1)}), bf16[8,2,128,640]{3,2,1,0:T(8,128)(2,1)}, u32[]{:S(2)}, u32[]{:S(2)}) async-start(bf16[8,2,128,640]{3,2,1,0:T(8,128)(2,1)} %bitcast.32), calls=%async_computation.2 | async-start | bytes 5242880 | tf_op jit(solution)/shard_map/all_to_all | solution.py:89
Sparse Core Ops, SparseCore 0:
  63.3 76.7 reduce-scatter.1
  144.4 46.7 all-gather.1
where the time goes:
time: 309 us; the launch traced here: 308 us
  waiting for transfers between devices  155 us (50%)
  blocking collectives  62.9 us (20%)
  other arithmetic  33.1 us (11%)
  local copies, waits for them, and re-layouts  19.5 us (6%)
  between operations  15.9 us (5%)
  matrix products  11.7 us (4%)
  starting transfers between devices  9.76 us (3%)
    reduce_scatter x1, waiting for transfers between devices, body(): lax.psum_scatter(lax.dot_general(embeddings, tiles, (((1,), (1,)), ((), (...  75.9 us
    psum x1, blocking collectives, body(): loss = lax.psum(loss_part, ('dp', 'proto')) / total_rows  62.9 us
    all_gather x1, waiting for transfers between devices, body(): dz_block = lax.all_gather(dz_rows, 'dp', axis=0, tiled=True)  46.9 us
    all_to_all x1, waiting for transfers between devices, body(): lax.all_to_all(outgoing, 'proto', split_axis=0, concat_axis=0, tiled=True)  32.2 us
    scatter-add x1, other arithmetic, body(): accum = jnp.zeros((tiles_here, TILE, width), jnp.float32).at[select.resha...  10.5 us
    convert_element_type x1, other arithmetic, body(): grad_table = accum.reshape(tiles_here * TILE, width).astype(jnp.bfloat16)  7.1 us
  transfers between devices with their start and end apart: 4, of which 3 were waited for; matrix products, arithmetic and copies ran while one was open for 2% of the time, Pallas kernels for 0%

commit v1 on v0

--- a/solution.py
+++ b/solution.py
@@ -7,6 +7,12 @@
 D = 2560
 TILE = 128
 CAP = 2
+
+
+def joined_along(blocks, dim):
+    lengths = list(blocks.shape[1:])
+    lengths[dim] *= blocks.shape[0]
+    return jnp.moveaxis(blocks, 0, dim).reshape(lengths)
 
 
 def slot_plan(ids, tiles_here):
@@ -75,7 +81,19 @@
     )
     my_labels = lax.dynamic_slice_in_dim(labels, part * rows_dev, rows_dev, 0)
     loss_part, dz_rows = softmax_terms(scores, my_ids, my_labels, list_len)
-    dz_block = lax.all_gather(dz_rows, "dp", axis=0, tiled=True)
+    peers = lax.axis_size("dp")
+    pairs = [(i, (i + 1) % peers) for i in range(peers)]
+    back = [(b, a) for a, b in pairs]
+    lower, upper = ([], [])
+    for step in range(peers - 1):
+        if step % 2 == 0:
+            lower.append(lax.ppermute(lower[-1] if lower else dz_rows, "dp", pairs))
+        else:
+            upper.append(lax.ppermute(upper[-1] if upper else dz_rows, "dp", back))
+    blocks = jnp.stack([*lower[::-1], dz_rows, *upper])
+    shift = lax.axis_index("dp") - len(lower)
+    blocks = blocks[(jnp.arange(peers) - shift) % peers]
+    dz_block = joined_along(blocks, 0)
     loss = lax.psum(loss_part, ("dp", "proto")) / total_rows
     grad_emb = jnp.dot(dz_block, tiles, preferred_element_type=jnp.float32).astype(jnp.bfloat16)
     piece = lax.dot_general(

time: 309 us -> 305 us (0.987)
  waiting for transfers between devices: 155 us -> 133 us
  starting transfers between devices: 9.76 us -> 22.6 us
  local copies, waits for them, and re-layouts: 19.5 us -> 23.5 us
    all_gather x1 -> x0, waiting for transfers between devices: 46.9 us -> none  [body(): dz_block = lax.all_gather(dz_rows, 'dp', axis=0, tiled=True)]
    ppermute x0 -> x3, waiting for transfers between devices: none -> 24.9 us  [the longest x2 23.7 us: body(): lower.append(lax.ppermute(lower[-1] if lower else dz_rows, 'dp', pairs))]
    ppermute x0 -> x3, starting transfers between devices: none -> 12.9 us  [the longest x2 10.5 us: body(): lower.append(lax.ppermute(lower[-1] if lower else dz_rows, 'dp', pairs))]
    gather x0 -> x2, local copies, waits for them, and re-layouts: none -> 4.98 us  [body(): blocks = blocks[(jnp.arange(peers) - shift) % peers]]
  transfers between devices with their start and end apart: 4 -> 6, of which waited for: 3 -> 5; matrix products, arithmetic and copies ran while one was open for 2% -> 3% of each run, Pallas kernels for 0% -> 0%
where the time goes in v1:
time: 305 us; the launch traced here: 304 us
  waiting for transfers between devices  133 us (44%)
  blocking collectives  61.6 us (20%)
  other arithmetic  35.6 us (12%)
  local copies, waits for them, and re-layouts  23.5 us (8%)
  starting transfers between devices  22.6 us (7%)
  between operations  16 us (5%)
  matrix products  11.5 us (4%)
    reduce_scatter x1, waiting for transfers between devices, body(): lax.psum_scatter(lax.dot_general(embeddings, tiles, (((1,), (1,)), ((), (...  75.9 us
    psum x1, blocking collectives, body(): loss = lax.psum(loss_part, ('dp', 'proto')) / total_rows  61.6 us
    all_to_all x1, waiting for transfers between devices, body(): lax.all_to_all(outgoing, 'proto', split_axis=0, concat_axis=0, tiled=True)  32.2 us
    ppermute x2, waiting for transfers between devices, body(): lower.append(lax.ppermute(lower[-1] if lower else dz_rows, 'dp', pairs))  23.7 us
    ppermute x2, starting transfers between devices, body(): lower.append(lax.ppermute(lower[-1] if lower else dz_rows, 'dp', pairs))  10.5 us
    scatter-add x1, other arithmetic, body(): accum = jnp.zeros((tiles_here, TILE, width), jnp.float32).at[select.resha...  10.5 us
    convert_element_type x1, other arithmetic, body(): grad_table = accum.reshape(tiles_here * TILE, width).astype(jnp.bfloat16)  7.1 us
  transfers between devices with their start and end apart: 6, of which 5 were waited for; matrix products, arithmetic and copies ran while one was open for 3% of the time, Pallas kernels for 0%

profile of v1, /device:TPU:0, one launch (start us, length us, event | category | flops | bytes accessed | tf_op | source)
XLA Modules:
  0.0 303.9 jit_solution(1479294771423388499)
XLA Ops:
  7.2 0.8 add_select_fusion
  8.0 0.7 broadcast_compare_fusion
  9.4 4.8 %gather_fusion = bf16[16,128,640]{2,1,0:T(8,128)(2,1)} fusion(bf16[32,128,640]{2,1,0:T(8,128)(2,1)} %bitcast.47, s32[1024]{0:T(1024)S(1)} %pad_clamp_fusion.2), kind=kCustom, calls=%fused_computation | custom fusion | bytes 5242944 | tf_op jit(solution)/shard_map/jit(_take)/gather | solution.py:62
  14.3 3.6 %broadcast_select_fusion = bf16[8,2,128,640]{3,2,1,0:T(8,128)(2,1)} fusion(bf16[8,2,128,640]{3,2,1,0:T(8,128)(2,1)} %bitcast.42, pred[8,2]{1,0:T(8,128)(4,1)S(1)} %copy.8), kind=kLoop, calls=%fused_computation.6 | loop fusion | flops 1310720 | bytes 5242896 | tf_op jit(solution)/shard_map/jit(_take)/select_n | solution.py:62
  17.8 5.2 %all-to-all-start = ((bf16[8,2,128,640]{3,2,1,0:T(8,128)(2,1)}), bf16[8,2,128,640]{3,2,1,0:T(8,128)(2,1)}, u32[]{:S(2)}, u32[]{:S(2)}) async-start(bf16[8,2,128,640]{3,2,1,0:T(8,128)(2,1)} %broadcast_select_fusion), calls=%async_computation | async-start | bytes 5242880 | tf_op jit(solution)/shard_map/all_to_all | solution.py:63
  23.2 32.2 %all-to-all-done = bf16[8,2,128,640]{3,2,1,0:T(8,128)(2,1)} async-done(((bf16[8,2,128,640]{3,2,1,0:T(8,128)(2,1)}), bf16[8,2,128,640]{3,2,1,0:T(8,128)(2,1)}, u32[]{:S(2)}, u32[]{:S(2)}) %all-to-all-start) | async-done | bytes 2621472 | tf_op jit(solution)/shard_map/all_to_all | solution.py:63
  55.4 2.5 gather_fusion.1
  58.2 3.8 %convolution_bitcast_fusion = f32[1024,1024]{0,1:T(8,128)} fusion(bf16[1024,640]{1,0:T(8,128)(2,1)S(1)} %bitcast_select_fusion, bf16[1024,640]{1,0:T(8,128)(2,1)S(1)} %copy-done), kind=kOutput, calls=%fused_computation.7 | convolution fusion | flops 1342177280 | bytes 6815744 | tf_op jit(solution)/shard_map/dot_general | solution.py:73
  62.1 0.7 fusion.7
  63.1 75.9 %reduce-scatter.2.cloned.1.call-done = f32[256,1024]{0,1:T(8,128)} async-done(((f32[1024,1024]{0,1:T(8,128)}), f32[256,1024]{0,1:T(8,128)}) %reduce-scatter.2.cloned.1.call-update) | async-done | bytes 1048592 | tf_op jit(solution)/shard_map/reduce_scatter | solution.py:72
  139.0 1.5 multiply_reduce_fusion
  140.5 1.5 fusion
  142.4 1.5 collective-permute-start
  143.9 2.3 collective-permute-start.2
  146.3 12.8 %collective-permute-done = bf16[256,1024]{0,1:T(8,128)(2,1)S(1)} collective-permute-done((bf16[256,1024]{0,1:T(8,128)(2,1)S(1)}, bf16[256,1024]{0,1:T(8,128)(2,1)S(1)}, u32[]{:S(2)}, u32[]{:S(2)}) %collective-permute-start) | collective-permute-done | bytes 524320 | tf_op jit(solution)/shard_map/ppermute | solution.py:90
  159.1 9.0 %collective-permute-start.1 = (bf16[256,1024]{0,1:T(8,128)(2,1)S(1)}, bf16[256,1024]{0,1:T(8,128)(2,1)}, u32[]{:S(2)}, u32[]{:S(2)}) collective-permute-start(bf16[256,1024]{0,1:T(8,128)(2,1)S(1)} %collective-permute-done), channel_id=1, source_target_pairs={{0,8},{8,16},{16,24},{24,0},{1,9},{9,17},{17,25},{25,1},{2,10},{10... | collective-permute-start | bytes 1572872 | tf_op jit(solution)/shard_map/ppermute | solution.py:90
  168.5 1.3 collective-permute-done.2
  169.7 10.9 %collective-permute-done.1 = bf16[256,1024]{0,1:T(8,128)(2,1)} collective-permute-done((bf16[256,1024]{0,1:T(8,128)(2,1)S(1)}, bf16[256,1024]{0,1:T(8,128)(2,1)}, u32[]{:S(2)}, u32[]{:S(2)}) %collective-permute-start.1) | collective-permute-done | bytes 524320 | tf_op jit(solution)/shard_map/ppermute | solution.py:90
  180.6 1.6 pad_maximum_fusion
  182.2 2.0 gather_fusion.2
  184.2 3.0 copy.10
  187.2 2.9 convolution_convert_fusion
  190.1 1.8 broadcast_in_dim.62
  191.9 3.1 %scatter_fusion = bf16[16,128,640]{2,1,0:T(8,128)(2,1)} fusion(bf16[16,128,640]{2,1,0:T(8,128)(2,1)} %broadcast_in_dim.62, s32[8]{0:T(128)S(1)} %fusion.10, bf16[8,128,640]{2,1,0:T(8,128)(2,1)S(1)} %bitcast.46), kind=kCustom, calls=%fused_computation.3 | custom fusion | bytes 3932192 | tf_op jit(solution)/shard_map/scatter | solution.py:105
  195.0 4.5 %all-to-all-start.1 = ((bf16[8,2,128,640]{3,2,1,0:T(8,128)(2,1)}), bf16[8,2,128,640]{3,2,1,0:T(8,128)(2,1)}, u32[]{:S(2)}, u32[]{:S(2)}) async-start(bf16[8,2,128,640]{3,2,1,0:T(8,128)(2,1)} %bitcast.41), calls=%async_computation.2 | async-start | bytes 5242880 | tf_op jit(solution)/shard_map/all_to_all | solution.py:107
  200.1 1.3 broadcast_select_fusion.1
  201.4 61.6 %psum.7 = f32[]{:T(128)} all-reduce(f32[]{:T(128)} %subtract_reduce_fusion), channel_id=1, replica_groups=mesh['dp'=4,'proto'=8] {'dp','proto'}, use_global_device_ids=true, to_apply=%region_8.9 | all-reduce | flops 1 | bytes 8 | tf_op jit(solution)/shard_map/psum | solution.py:97
  263.7 4.8 %convolution_convert_fusion.1 = bf16[1024,640]{1,0:T(8,128)(2,1)} fusion(bf16[1024,1024]{1,0:T(8,128)(2,1)} %bitcast.45, bf16[1024,640]{1,0:T(8,128)(2,1)} %bitcast.48), kind=kOutput, calls=%fused_computation.10 | convolution fusion | flops 1342832640 | bytes 4718592 | tf_op jit(solution)/shard_map/dot_general | solution.py:98
  268.5 4.6 %bitcast_convert_fusion = f32[16,128,640]{2,1,0:T(8,128)} fusion(bf16[8,2,128,640]{3,2,1,0:T(8,128)(2,1)} %all-to-all-done.1), kind=kLoop, calls=%fused_computation.5 | loop fusion | flops 1310720 | bytes 7864320 | tf_op jit(solution)/shard_map/convert_element_type | solution.py:117
  273.1 5.2 %broadcast_in_dim.61 = f32[32,128,640]{2,1,0:T(8,128)} broadcast(f32[]{:T(128)} %constant.131.clone.1), dimensions={} | broadcast | bytes 10485764 | tf_op jit(solution)/shard_map/broadcast_in_dim | solution.py:115
  278.3 10.5 %scatter_fusion.1 = f32[32,128,640]{2,1,0:T(8,128)} fusion(f32[32,128,640]{2,1,0:T(8,128)} %broadcast_in_dim.61, s32[16]{0:T(128)S(1)} %fusion.9, f32[16,128,640]{2,1,0:T(8,128)} %bitcast_convert_fusion), kind=kCustom, calls=%fused_computation.4 | custom fusion | flops 1310720 | bytes 15728704 | tf_op jit(solution)/shard_map/scatter-add | solution.py:117
  288.8 7.1 %convert_element_type.36 = bf16[32,128,640]{2,1,0:T(8,128)(2,1)} convert(f32[32,128,640]{2,1,0:T(8,128)} %scatter_fusion.1) | non-fusion elementwise | flops 2621440 | bytes 15728640 | tf_op jit(solution)/shard_map/convert_element_type | solution.py:119
  (41 shorter events, 2.8 us)
Async XLA Ops:
  7.2 51.1 %copy-start = (bf16[1024,640]{1,0:T(8,128)(2,1)S(1)}, bf16[1024,640]{1,0:T(8,128)(2,1)}, u32[]{:S(2)}) copy-start(bf16[1024,640]{1,0:T(8,128)(2,1)} %param.4) | copy-start | bytes 3932164
  17.8 37.5 %all-to-all-start = ((bf16[8,2,128,640]{3,2,1,0:T(8,128)(2,1)}), bf16[8,2,128,640]{3,2,1,0:T(8,128)(2,1)}, u32[]{:S(2)}, u32[]{:S(2)}) async-start(bf16[8,2,128,640]{3,2,1,0:T(8,128)(2,1)} %broadcast_select_fusion), calls=%async_computation | async-start | bytes 5242880 | tf_op jit(solution)/shard_map/all_to_all | solution.py:63
  23.0 116.0 %reduce-scatter.2.cloned.1.call-start = ((), (), s32[]{:S(2)}) async-start(), calls=%async_computation.3 | async-start | bytes 5242880 | tf_op jit(solution)/shard_map/reduce_scatter | solution.py:72
  57.9 4.2 %copy-start.2 = (bf16[8,128,640]{2,1,0:T(8,128)(2,1)}, bf16[8,128,640]{2,1,0:T(8,128)(2,1)S(1)}, u32[]{:S(2)}) copy-start(bf16[8,128,640]{2,1,0:T(8,128)(2,1)S(1)} %gather_fusion.1) | copy-start | bytes 3932164
  62.1 0.7 copy-start.7
  139.0 3.0 copy-start.1
  142.4 16.7 %collective-permute-start = (bf16[256,1024]{0,1:T(8,128)(2,1)S(1)}, bf16[256,1024]{0,1:T(8,128)(2,1)S(1)}, u32[]{:S(2)}, u32[]{:S(2)}) collective-permute-start(bf16[256,1024]{0,1:T(8,128)(2,1)S(1)} %subtract_convert_fusion), channel_id=1, source_target_pairs={{0,8},{8,16},{16,24},{24,0},{1,9},{9,17},{17,25},{25,1},{2,10},{10... | collective-permute-start | bytes 1572872 | tf_op jit(solution)/shard_map/ppermute | solution.py:90
  143.9 25.8 %collective-permute-start.2 = (bf16[256,1024]{0,1:T(8,128)(2,1)S(1)}, bf16[256,1024]{0,1:T(8,128)(2,1)}, u32[]{:S(2)}, u32[]{:S(2)}) collective-permute-start(bf16[256,1024]{0,1:T(8,128)(2,1)S(1)} %subtract_convert_fusion), channel_id=1, source_target_pairs={{8,0},{16,8},{24,16},{0,24},{9,1},{17,9},{25,17},{1,25},{10,2},{18... | collective-permute-start | bytes 1572872 | tf_op jit(solution)/shard_map/ppermute | solution.py:92
  159.1 21.5 %copy-start.6 = (bf16[256,1024]{0,1:T(8,128)(2,1)}, bf16[256,1024]{0,1:T(8,128)(2,1)S(1)}, u32[]{:S(2)}) copy-start(bf16[256,1024]{0,1:T(8,128)(2,1)S(1)} %collective-permute-done) | copy-start | bytes 1572868
  159.1 21.5 %collective-permute-start.1 = (bf16[256,1024]{0,1:T(8,128)(2,1)S(1)}, bf16[256,1024]{0,1:T(8,128)(2,1)}, u32[]{:S(2)}, u32[]{:S(2)}) collective-permute-start(bf16[256,1024]{0,1:T(8,128)(2,1)S(1)} %collective-permute-done), channel_id=1, source_target_pairs={{0,8},{8,16},{16,24},{24,0},{1,9},{9,17},{17,25},{25,1},{2,10},{10... | collective-permute-start | bytes 1572872 | tf_op jit(solution)/shard_map/ppermute | solution.py:90
  187.2 2.9 copy-start.4
  190.1 1.8 copy-start.5
  195.0 5.1 %copy-start.3 = (bf16[8,128,640]{2,1,0:T(8,128)(2,1)S(1)}, bf16[8,128,640]{2,1,0:T(8,128)(2,1)}, u32[]{:S(2)}) copy-start(bf16[8,128,640]{2,1,0:T(8,128)(2,1)} %copy-done.2) | copy-start | bytes 3932164
  195.0 73.5 %all-to-all-start.1 = ((bf16[8,2,128,640]{3,2,1,0:T(8,128)(2,1)}), bf16[8,2,128,640]{3,2,1,0:T(8,128)(2,1)}, u32[]{:S(2)}, u32[]{:S(2)}) async-start(bf16[8,2,128,640]{3,2,1,0:T(8,128)(2,1)} %bitcast.41), calls=%async_computation.2 | async-start | bytes 5242880 | tf_op jit(solution)/shard_map/all_to_all | solution.py:107
Sparse Core Ops, SparseCore 0:
  62.2 76.7 reduce-scatter.1
